TPU v7x, 32 devices: a whole 2x2x4 slice. The times are simulated.
32 devices in a mesh: gx: 4 (over x, core), gy: 8 (over z, y).
Axes of the slice: x: 2, y: 2, z: 4, core: 2. Of those that a mesh axis runs over, the one named last changes fastest.
Arguments:
- phase_field: float32 [16, 2048, 2048], P(None, 'gy', 'gx'), may hold values from -1 to 1
- mobility: float32 [16, 2048, 2048], P(None, 'gy', 'gx'), may hold values from 0.25 to 2.5
- x_inverse: bfloat16 [2048, 2048], P('gx'), may hold values from -2 to 2
- y_inverse: bfloat16 [2048, 2048], P('gy'), may hold values from -2 to 2
Outputs:
- new_phase: float32 [16, 2048, 2048], P(None, 'gy', 'gx')
All inputs are finite; a program needn't handle non-finite values.
Results may differ from a plain program's by a relative error of at most 0.0041.
Values may be sent and summed in bfloat16 or wider, within the bound.
A program may use at most 128 MiB of HBM per device.

v0:
```python
import jax
import jax.numpy as jnp
from jax import lax
from jax.sharding import PartitionSpec as P

step_size = 0.15


def extended(x, sides, width):
    for axis, dim in sides:
        size, length = (lax.axis_size(axis), x.shape[dim])
        up = [(i, (i + 1) % size) for i in range(size - 1)]
        down = [(j, i) for i, j in up]
        last = lax.slice_in_dim(x, length - width, length, axis=dim)
        leading = lax.slice_in_dim(x, 0, width, axis=dim)
        before = lax.ppermute(last, axis, up)
        after = lax.ppermute(leading, axis, down)
        x = jnp.concatenate([before, x, after], axis=dim)
    return x


def face_mob(center_mob, near_mob):
    return 2.0 * center_mob * near_mob / jnp.maximum(center_mob + near_mob, 0.25)


def laplace(values, mobile):
    values_z = jnp.pad(values, ((1, 1), (0, 0), (0, 0)))
    mobile_z = jnp.pad(mobile, ((1, 1), (0, 0), (0, 0)))
    center = values[:, 1:-1, 1:-1]
    center_mob = mobile[:, 1:-1, 1:-1]
    pairs = [
        (values_z[2:, 1:-1, 1:-1], mobile_z[2:, 1:-1, 1:-1]),
        (values_z[:-2, 1:-1, 1:-1], mobile_z[:-2, 1:-1, 1:-1]),
        (values[:, 2:, 1:-1], mobile[:, 2:, 1:-1]),
        (values[:, :-2, 1:-1], mobile[:, :-2, 1:-1]),
        (values[:, 1:-1, 2:], mobile[:, 1:-1, 2:]),
        (values[:, 1:-1, :-2], mobile[:, 1:-1, :-2]),
    ]
    result = jnp.zeros_like(center)
    for near_val, near_mob in pairs:
        result = result + face_mob(center_mob, near_mob) * (near_val - center)
    return result


def local(phase_field, mobility, x_inverse, y_inverse):
    whole_inverse = lax.all_gather(y_inverse, "gy", axis=0, tiled=True)
    stacked = jnp.stack((phase_field, mobility))
    padded = extended(stacked, (("gx", 3), ("gy", 2)), 1)
    mob_near = padded[1]
    first = phase_field + step_size * laplace(padded[0], mob_near)
    first_pad = extended(first, (("gx", 2), ("gy", 1)), 1)
    second = (first + step_size * laplace(first_pad, mob_near)).astype(jnp.bfloat16)
    planes, y_rows, x_rows = second.shape
    out_rows = x_inverse.shape[0]
    segment = lax.all_gather(second, "gx", axis=2, tiled=True)
    seg_len = segment.shape[2]
    flat = segment.reshape(planes * y_rows, seg_len)
    lines = lax.dot_general(
        flat, x_inverse, (((1,), (1,)), ((), ())), preferred_element_type=jnp.float32
    )
    solved = lines.reshape(planes, y_rows, out_rows)
    chemical = solved * solved * solved - solved
    chemical_pad = extended(chemical, (("gx", 2), ("gy", 1)), 1)
    updated = (solved + step_size * laplace(chemical_pad, mob_near)).astype(jnp.bfloat16)
    columns = jnp.transpose(updated, (1, 0, 2)).reshape(y_rows, planes * x_rows)
    line_block = lax.all_to_all(columns, "gy", split_axis=1, concat_axis=0, tiled=True)
    solved_cols = jnp.dot(whole_inverse, line_block, preferred_element_type=jnp.float32)
    returned = lax.all_to_all(solved_cols, "gy", split_axis=0, concat_axis=1, tiled=True)
    return jnp.transpose(returned.reshape(y_rows, planes, x_rows), (1, 0, 2))


def solution(mesh):
    placed = (P(None, "gy", "gx"), P(None, "gy", "gx"), P("gx", None), P("gy", None))
    return jax.shard_map(
        local, mesh=mesh, in_specs=placed, out_specs=P(None, "gy", "gx"), check_vma=False
    )
```

profile of v0, /device:TPU:0, one launch (start us, length us, event | category | flops | bytes accessed | tf_op | source)
XLA Modules:
  0.0 789.2 jit_solution(2663590214794655150)
XLA Ops:
  7.4 8.2 %pad_maximum_fusion.18 = (f32[2,16,256,1]{3,2,1,0:T(8,128)}, f32[2,16,256,1]{3,2,1,0:T(8,128)}) fusion(f32[1,16,256,512]{3,2,1,0:T(8,128)} %bitcast.36, f32[1,16,256,512]{3,2,1,0:T(8,128)} %bitcast.33), kind=kLoop, calls=%fused_computation.102 | loop fusion | flops 16384 | bytes 16842752 | tf_op jit(solution)/shard_map/slice | solution.py:14
  15.6 2.8 copy.9
  18.4 2.4 collective-permute-start
  20.8 2.8 copy.10
  24.9 2.7 copy.11
  28.8 2.7 copy.12
  33.6 3.7 collective-permute-start.2
  39.3 4.3 collective-permute-done.3
  43.6 19.0 %pad_maximum_fusion = f32[2,16,258,514]{3,2,1,0:T(8,128)} fusion(f32[2,16,1,514]{3,2,1,0:T(1,128)S(1)} %collective-permute-done.3, f32[2,16,256,1]{3,2,1,0:T(8,128)S(1)} %copy-done.4, f32[1,16,256,512]{3,2,1,0:T(8,128)} %bitcast.38, f32[1,16,256,512]{3,2,1,0:T(8,128)} %bitcast.35, f32[2,16,256,1]{3,2,1,0:T(8,128)S(1)} %copy-done.3, ...), kind=kLoop, calls=%fused_computation | loop fusion | flops 21217920 | bytes 33948672 | tf_op jit(solution)/shard_map/concatenate | solution.py:18
  62.6 12.3 %slice_bitcast_fusion.1 = (f32[16,258,514]{2,1,0:T(8,128)S(1)}, f32[16,258,514]{2,1,0:T(8,128)}) fusion(f32[2,16,258,514]{3,2,1,0:T(8,128)} %pad_maximum_fusion), kind=kLoop, calls=%fused_computation.18 | loop fusion | bytes 33948672 | tf_op jit(solution)/shard_map/squeeze | solution.py:49
  74.9 43.0 %fusion.9 = f32[16,256,512]{2,1,0:T(8,128)} fusion(f32[16,256,512]{2,1,0:T(8,128)} %param.4, f32[16,258,514]{2,1,0:T(8,128)} %get-tuple-element.8, f32[16,258,514]{2,1,0:T(8,128)S(1)} %get-tuple-element.7), kind=kLoop, calls=%fused_computation.27 | loop fusion | flops 92274688 | bytes 122290176 | tf_op jit(solution)/shard_map/add | solution.py:50
  117.9 5.0 fusion.56
  122.9 2.2 copy.13
  125.1 3.6 collective-permute-start.4
  128.7 2.2 copy.14
  139.5 4.3 collective-permute-start.6
  145.5 4.7 collective-permute-done.7
  150.2 12.2 %select_maximum_fusion.4 = f32[18,258,514]{2,1,0:T(8,128)} fusion(f32[16,1,514]{2,1,0:T(1,128)S(1)} %collective-permute-done.7, f32[16,1,514]{2,1,0:T(1,128)S(1)} %collective-permute-done.6, f32[16,256,1]{2,1,0:T(8,128)S(1)} %copy-done.8, f32[16,256,512]{2,1,0:T(8,128)} %fusion.9, f32[16,256,1]{2,1,0:T(8,128)S(1)} %copy-done.7), kind=kLoop, calls=%fused_computation.8 | loop fusion | flops 28644192 | bytes 18035232 | tf_op jit(solution)/shard_map/concatenate | solution.py:18
  162.4 43.8 %fusion.35 = bf16[16,256,512]{2,1,0:T(8,128)(2,1)} fusion(f32[16,256,512]{2,1,0:T(8,128)} %fusion.9, f32[16,256,1]{2,1,0:T(8,128)} %copy.15, f32[16,256,1]{2,1,0:T(8,128)} %copy.16, f32[16,1,514]{2,1,0:T(1,128)S(1)} %collective-permute-done.6, f32[16,1,514]{2,1,0:T(1,128)S(1)} %collective-permute-done.7, f32[18,258,514]{2,1,0:T(8,128)} %select_maximum_fusion.4, ...), kind=kLoop, calls=%fused_computation.65 | loop fusion | flops 111149056 | bytes 82231296 | tf_op jit(solution)/shard_map/convert_element_type | solution.py:52
  206.4 107.5 %all-gather.3.cloned.1.call-done = bf16[16,256,2048]{2,1,0:T(8,128)(2,1)} async-done(((bf16[16,256,512]{2,1,0:T(8,128)(2,1)}), bf16[16,256,2048]{2,1,0:T(8,128)(2,1)}) %all-gather.3.cloned.1.call-update) | async-done | bytes 16777232 | tf_op jit(solution)/shard_map/all_gather | solution.py:55
  313.9 16.2 %multiply_subtract_fusion = (f32[16,256,512]{2,1,0:T(8,128)}, f32[16,256,512]{2,1,0:T(8,128)}) fusion(bf16[16,256,2048]{2,1,0:T(8,128)(2,1)} %all-gather.3.cloned.1.call-done, bf16[512,2048]{1,0:T(8,128)(2,1)S(1)} %copy-done), kind=kOutput, calls=%fused_computation.3 | convolution fusion | flops 8596226048 | bytes 35651584 | tf_op jit(solution)/shard_map/dot_general | solution.py:58
  330.2 4.4 fusion.55
  346.0 3.4 collective-permute-start.10
  351.1 4.3 collective-permute-done.11
  355.3 14.8 %select_maximum_fusion = f32[18,258,514]{2,1,0:T(8,128)} fusion(f32[16,1,514]{2,1,0:T(1,128)S(1)} %collective-permute-done.11, f32[16,1,514]{2,1,0:T(1,128)S(1)} %collective-permute-done.10, f32[16,256,1]{2,1,0:T(8,128)} %copy.22, f32[16,256,512]{2,1,0:T(8,128)} %get-tuple-element.19, f32[16,256,1]{2,1,0:T(8,128)} %copy-done.5), kind=kLoop, calls=%fused_computation.4 | loop fusion | flops 28644192 | bytes 18035232 | tf_op jit(solution)/shard_map/concatenate | solution.py:18
  370.2 43.7 %fusion.52 = bf16[256,16,512]{2,0,1:T(8,128)(2,1)} fusion(f32[16,256,512]{2,1,0:T(8,128)} %get-tuple-element.20, f32[16,256,512]{2,1,0:T(8,128)} %get-tuple-element.19, f32[16,256,1]{2,1,0:T(8,128)S(1)} %copy-done.6, f32[16,256,1]{2,1,0:T(8,128)} %copy.22, f32[16,1,514]{2,1,0:T(1,128)S(1)} %collective-permute-done.10, ...), kind=kLoop, calls=%fused_computation.103 | loop fusion | flops 111149056 | bytes 92700672 | tf_op jit(solution)/shard_map/transpose | solution.py:65
  413.9 6.4 copy.25
  420.3 145.2 %all_to_all.35 = bf16[256,8,1024]{0,2,1:T(8,128)(2,1)} all-to-all(bf16[256,8,1024]{0,2,1:T(8,128)(2,1)} %bitcast.41), channel_id=1, replica_groups=mesh['gx'=4,'gy'=8] {'gy'}, dimensions={1} | all-to-all | bytes 8388608 | tf_op jit(solution)/shard_map/all_to_all | solution.py:66
  565.5 6.4 copy.26
  572.0 12.6 %fusion.57 = f32[1024,2048]{1,0:T(8,128)S(1)} fusion(bf16[2048,1024]{1,0:T(8,128)(2,1)} %bitcast.44, bf16[2048,2048]{1,0:T(8,128)(2,1)} %all-gather.5.cloned.1.call-done), kind=kOutput, calls=%fused_computation.118 | convolution fusion | flops 8589934592 | bytes 20971520 | tf_op jit(solution)/shard_map/dot_general | solution.py:67
  585.3 186.8 %all_to_all.36 = f32[8,256,1024]{1,2,0:T(8,128)} all-to-all(f32[8,256,1024]{1,2,0:T(8,128)S(1)} %bitcast.39), channel_id=1, replica_groups=mesh['gx'=4,'gy'=8] {'gy'}, dimensions={0} | all-to-all | bytes 16777216 | tf_op jit(solution)/shard_map/all_to_all | solution.py:68
  772.1 9.4 %copy.28 = f32[16,256,512]{2,1,0:T(8,128)} copy(f32[16,256,512]{1,2,0:T(8,128)} %bitcast.40) | data formatting | bytes 16777216 | tf_op jit(solution)/shard_map/transpose | solution.py:69
  (63 shorter events, 31.0 us)
Async XLA Ops:
  7.4 306.6 %copy-start = (bf16[512,2048]{1,0:T(8,128)(2,1)S(1)}, bf16[512,2048]{1,0:T(8,128)(2,1)}, u32[]{:S(2)}) copy-start(bf16[512,2048]{1,0:T(8,128)(2,1)} %param.6) | copy-start | bytes 6291460
  7.4 306.6 %all-gather.3.cloned.1.call-start = ((), (), s32[]{:S(2)}) async-start(), calls=%async_computation.2 | async-start | bytes 20971520 | tf_op jit(solution)/shard_map/all_gather | solution.py:55
  18.4 6.5 collective-permute-start
  23.6 5.2 collective-permute-start.1
  31.5 12.1 %copy-start.3 = (f32[2,16,256,1]{3,2,1,0:T(8,128)S(1)}, f32[2,16,256,1]{3,2,1,0:T(8,128)}, u32[]{:S(2)}) copy-start(f32[2,16,256,1]{3,2,1,0:T(8,128)} %copy.11) | copy-start | bytes 98308
  31.5 12.1 %copy-start.4 = (f32[2,16,256,1]{3,2,1,0:T(8,128)S(1)}, f32[2,16,256,1]{3,2,1,0:T(8,128)}, u32[]{:S(2)}) copy-start(f32[2,16,256,1]{3,2,1,0:T(8,128)} %copy.12) | copy-start | bytes 98308
  33.6 5.7 collective-permute-start.2
  37.3 6.3 collective-permute-start.3
  74.9 43.0 %copy-start.2 = (f32[16,258,514]{2,1,0:T(8,128)}, f32[16,258,514]{2,1,0:T(8,128)S(1)}, u32[]{:S(2)}) copy-start(f32[16,258,514]{2,1,0:T(8,128)S(1)} %get-tuple-element.7) | copy-start | bytes 25461508
  125.1 7.1 collective-permute-start.4
  130.9 5.1 collective-permute-start.5
  138.0 12.2 %copy-start.7 = (f32[16,256,1]{2,1,0:T(8,128)S(1)}, f32[16,256,1]{2,1,0:T(8,128)}, u32[]{:S(2)}) copy-start(f32[16,256,1]{2,1,0:T(8,128)} %copy.15) | copy-start | bytes 49156
  138.0 12.2 %copy-start.8 = (f32[16,256,1]{2,1,0:T(8,128)S(1)}, f32[16,256,1]{2,1,0:T(8,128)}, u32[]{:S(2)}) copy-start(f32[16,256,1]{2,1,0:T(8,128)} %copy.16) | copy-start | bytes 49156
  139.5 6.0 collective-permute-start.6
  143.8 18.5 %slice-start = ((s8[10813440]{0:T(1024)(128)(4,1)}), s8[4194304]{0:T(1024)(128)(4,1)S(1)}, s32[]{:S(2)}) async-start(s8[10813440]{0:T(1024)(128)(4,1)} %bitcast.29), calls=%async_computation.4 | async-start | bytes 8388608
  143.8 18.5 %slice-start.1 = ((s8[10813440]{0:T(1024)(128)(4,1)}), s8[4194304]{0:T(1024)(128)(4,1)S(1)}, s32[]{:S(2)}) async-start(s8[10813440]{0:T(1024)(128)(4,1)} %bitcast.29), calls=%async_computation.5 | async-start | bytes 8388608
  143.8 18.5 %slice-start.2 = ((s8[10813440]{0:T(1024)(128)(4,1)}), s8[2424832]{0:T(1024)(128)(4,1)S(1)}, s32[]{:S(2)}) async-start(s8[10813440]{0:T(1024)(128)(4,1)} %bitcast.29), calls=%async_computation.6 | async-start | bytes 4849664
  143.9 6.3 collective-permute-start.7
  206.2 365.7 %all-gather.5.cloned.1.call-start = ((), (), s32[]{:S(2)}) async-start(), calls=%async_computation.3 | async-start | bytes 9437184 | tf_op jit(solution)/shard_map/all_gather | solution.py:46
  336.7 4.1 collective-permute-start.8
  339.5 3.1 collective-permute-start.9
  341.5 8.0 %copy-start.5 = (f32[16,256,1]{2,1,0:T(8,128)}, f32[16,256,1]{2,1,0:T(8,128)S(1)}, u32[]{:S(2)}) copy-start(f32[16,256,1]{2,1,0:T(8,128)S(1)} %copy.21) | copy-start | bytes 49156
  346.0 5.0 collective-permute-start.10
  349.4 5.9 collective-permute-start.11
  351.0 19.2 %slice-start.3 = ((s8[10813440]{0:T(1024)(128)(4,1)}), s8[2424832]{0:T(1024)(128)(4,1)S(1)}, s32[]{:S(2)}) async-start(s8[10813440]{0:T(1024)(128)(4,1)} %bitcast.31), calls=%async_computation.7 | async-start | bytes 4849664
  351.0 19.2 %slice-start.4 = ((s8[10813440]{0:T(1024)(128)(4,1)}), s8[4194304]{0:T(1024)(128)(4,1)S(1)}, s32[]{:S(2)}) async-start(s8[10813440]{0:T(1024)(128)(4,1)} %bitcast.31), calls=%async_computation.8 | async-start | bytes 8388608
  351.0 19.2 %slice-start.5 = ((s8[10813440]{0:T(1024)(128)(4,1)}), s8[4194304]{0:T(1024)(128)(4,1)S(1)}, s32[]{:S(2)}) async-start(s8[10813440]{0:T(1024)(128)(4,1)} %bitcast.31), calls=%async_computation.9 | async-start | bytes 8388608
  351.0 19.2 %copy-start.6 = (f32[16,256,1]{2,1,0:T(8,128)S(1)}, f32[16,256,1]{2,1,0:T(8,128)}, u32[]{:S(2)}) copy-start(f32[16,256,1]{2,1,0:T(8,128)} %copy-done.5) | copy-start | bytes 49156
  772.1 9.4 %copy-start.1 = (bf16[512,2048]{1,0:T(8,128)(2,1)S(1)}, bf16[512,2048]{1,0:T(8,128)(2,1)}, u32[]{:S(2)}) copy-start(bf16[512,2048]{1,0:T(8,128)(2,1)} %param.6) | copy-start | bytes 6291460
Sparse Core Ops, SparseCore 0:
  206.3 107.5 all-gather.2
Sparse Core Ops, SparseCore 1:
  351.1 193.4 all-gather.4
where the time goes:
time: 799 us; the launch traced here: 789 us
  blocking collectives  332 us (42%)
  other arithmetic  190 us (24%)
  waiting for transfers between devices  126 us (16%)
  local copies, waits for them, and re-layouts  69.5 us (9%)
  matrix products  28.8 us (4%)
  starting transfers between devices  28 us (4%)
  between operations  15.4 us (2%)
    all_to_all x1, blocking collectives, local(): lax.all_to_all(solved_cols, 'gy', split_axis=0, concat_axis=1, tiled=True)  187 us
    all_to_all x1, blocking collectives, local(): lax.all_to_all(columns, 'gy', split_axis=1, concat_axis=0, tiled=True)  145 us
    all_gather x1, waiting for transfers between devices, local(): segment = lax.all_gather(second, 'gx', axis=2, tiled=True)  107 us
    concatenate x5, other arithmetic, extended(): x = jnp.concatenate([before, x, after], axis=dim)  48.9 us
    convert_element_type x1, other arithmetic, local(): (first + step_size * laplace(first_pad, mob_near)).astype(jnp.bfloat16)  43.8 us
    transpose x1, other arithmetic, local(): columns = jnp.transpose(updated, (1, 0, 2)).reshape(y_rows, planes * x_rows)  43.7 us
    add x1, other arithmetic, local(): first = phase_field + step_size * laplace(padded[0], mob_near)  43 us
    ppermute x6, starting transfers between devices, extended(): before = lax.ppermute(last, axis, up)  19.6 us
  transfers between devices with their start and end apart: 14, of which 10 were waited for; matrix products, arithmetic and copies ran while one was open for 10% of the time, Pallas kernels for 0%

commit v1 on v0

--- a/solution.py
+++ b/solution.py
@@ -1,9 +1,20 @@
+import functools
+
 import jax
 import jax.numpy as jnp
 from jax import lax
+from jax.experimental import pallas as pl
+from jax.experimental.pallas import tpu as pltpu
 from jax.sharding import PartitionSpec as P
 
 step_size = 0.15
+PAD = 8
+STRIP = 32
+MESH = pl.DeviceIdType.MESH
+
+
+def face_mob(center_mob, near_mob):
+    return 2.0 * center_mob * near_mob / jnp.maximum(center_mob + near_mob, 0.25)
 
 
 def extended(x, sides, width):
@@ -17,10 +28,6 @@
         after = lax.ppermute(leading, axis, down)
         x = jnp.concatenate([before, x, after], axis=dim)
     return x
-
-
-def face_mob(center_mob, near_mob):
-    return 2.0 * center_mob * near_mob / jnp.maximum(center_mob + near_mob, 0.25)
 
 
 def laplace(values, mobile):
@@ -42,7 +49,7 @@
     return result
 
 
-def local(phase_field, mobility, x_inverse, y_inverse):
+def plain(phase_field, mobility, x_inverse, y_inverse):
     whole_inverse = lax.all_gather(y_inverse, "gy", axis=0, tiled=True)
     stacked = jnp.stack((phase_field, mobility))
     padded = extended(stacked, (("gx", 3), ("gy", 2)), 1)
@@ -53,8 +60,7 @@
     planes, y_rows, x_rows = second.shape
     out_rows = x_inverse.shape[0]
     segment = lax.all_gather(second, "gx", axis=2, tiled=True)
-    seg_len = segment.shape[2]
-    flat = segment.reshape(planes * y_rows, seg_len)
+    flat = segment.reshape(planes * y_rows, segment.shape[2])
     lines = lax.dot_general(
         flat, x_inverse, (((1,), (1,)), ((), ())), preferred_element_type=jnp.float32
     )
@@ -69,8 +75,527 @@
     return jnp.transpose(returned.reshape(y_rows, planes, x_rows), (1, 0, 2))
 
 
+def half_mob(center_mob, near_mob):
+    total = jnp.maximum(center_mob + near_mob, 0.25)
+    inverse = pl.reciprocal(total, approx=True)
+    inverse = inverse * (2.0 - total * inverse)
+    return center_mob * near_mob * inverse
+
+
+def sweep_plane(z, v, m, above, cols, chemical, y_rows, width, store):
+    def flux_down(r, n):
+        tall_v, tall_m = chemical(v[z, pl.ds(r, n + PAD), :]), m[z, pl.ds(r, n + PAD), :]
+        low_v, low_m = pltpu.roll(tall_v, n + PAD - 1, 0)[:n], pltpu.roll(tall_m, n + PAD - 1, 0)[:n]
+        return half_mob(tall_m[:n], low_m) * (low_v - tall_v[:n]), tall_v[:n], tall_m[:n]
+
+    def strip(i, carried):
+        r = pl.multiple_of(i * STRIP, STRIP)
+        inner, mine = pl.ds(r + PAD, STRIP), pl.ds(r, STRIP)
+        down, own, mob = flux_down(r + PAD, STRIP)
+        stacked = jnp.concatenate([carried, down], axis=0)
+        total = down - pltpu.roll(stacked, 1, 0)[PAD:]
+        below = half_mob(mob, m[z + 1, inner, :]) * (chemical(v[z + 1, inner, :]) - own)
+        total = total + (below - above[mine, :])
+        above[mine, :] = below
+        v_left, v_right, m_left, m_right = cols(z, mine)
+        lane = lax.broadcasted_iota(jnp.int32, own.shape, 1)
+        at_end = lane == width - 1
+        v_next = jnp.where(at_end, v_right, pltpu.roll(own, width - 1, 1))
+        m_next = jnp.where(at_end, m_right, pltpu.roll(mob, width - 1, 1))
+        flux = half_mob(mob, m_next) * (v_next - own)
+        entering = half_mob(m_left, mob[:, 0:1]) * (own[:, 0:1] - v_left)
+        total = total + (flux - jnp.where(lane == 0, entering, pltpu.roll(flux, 1, 1)))
+        store(mine, inner, total)
+        return down[STRIP - PAD:]
+
+    first_carry, _, _ = flux_down(0, PAD)
+    lax.fori_loop(0, y_rows // STRIP, strip, first_carry)
+
+
+def step_kernel(
+    nx, ny, stages, w,
+    phase, mobility, x_hbm, y_hbm, out, gath,
+    v, m, f, second, gbuf, xsrc, xt, yinv, upd, yrecv, above, e1, r1, e2, r2,
+    load_sems, row_send, row_recv, col_send, col_recv, xr_send, xr_recv,
+    y_send, y_recv, gx_send, gx_recv, pair_send, pair_recv, sol_send, sol_recv,
+    a2a_send, a2a_recv, ret_send, ret_recv, keep_sems, g_sems,
+):
+    planes, y_rows, width = phase.shape
+    gx, gy = lax.axis_index("gx"), lax.axis_index("gy")
+    partner = gx + 1 - 2 * lax.rem(gx, 2)
+    mate = gy + 1 - 2 * lax.rem(gy, 2)
+    side_half = lax.rem(gx, 2)
+    half, y_half = nx // 2, ny // 2
+    per = len(stages)
+    chunk = planes // per
+    cuts = width // w
+    depth = y_rows // 2
+    every = pl.ds(0, planes)
+
+    def remote(src, dst, send, recv, x_to, y_to):
+        return pltpu.make_async_remote_copy(
+            src, dst, send, recv, device_id=(x_to, y_to), device_id_type=MESH)
+
+    barrier = pltpu.get_barrier_semaphore()
+    for d in range(1, ny):
+        pl.semaphore_signal(barrier, inc=1, device_id=(gx, lax.rem(gy + d, ny)), device_id_type=MESH)
+    for d in range(1, nx):
+        pl.semaphore_signal(barrier, inc=1, device_id=(lax.rem(gx + d, nx), gy), device_id_type=MESH)
+
+    loads = [
+        pltpu.make_async_copy(phase, v.at[every, pl.ds(PAD, y_rows), :], load_sems.at[0]),
+        pltpu.make_async_copy(mobility, m.at[every, pl.ds(PAD, y_rows), :], load_sems.at[1]),
+        pltpu.make_async_copy(x_hbm, xsrc.at[pl.ds(0, width), :], load_sems.at[2]),
+        pltpu.make_async_copy(y_hbm.at[pl.ds(0, depth), :], yinv.at[gy, 0], load_sems.at[3]),
+        pltpu.make_async_copy(y_hbm.at[pl.ds(depth, depth), :], yinv.at[gy, 1], load_sems.at[4]),
+    ]
+    for copy in loads:
+        copy.start()
+
+    up_ok, down_ok = gy > 0, gy < ny - 1
+    left_ok, right_ok = gx > 0, gx < nx - 1
+
+    @pl.when(gy == 0)
+    def _():
+        for ref in (v, m, f):
+            ref[every, pl.ds(0, PAD), :] = jnp.zeros((planes, PAD, width), jnp.float32)
+
+    @pl.when(gy == ny - 1)
+    def _():
+        for ref in (v, m, f):
+            ref[every, pl.ds(PAD + y_rows, PAD), :] = jnp.zeros((planes, PAD, width), jnp.float32)
+
+    @pl.when(gx == 0)
+    def _():
+        for ref in (r1, r2):
+            ref[0] = jnp.zeros(ref.shape[1:], jnp.float32)
+        xsrc[pl.ds(width, 16), :] = jnp.zeros((16, xsrc.shape[1]), xsrc.dtype)
+
+    @pl.when(gx == nx - 1)
+    def _():
+        for ref in (r1, r2):
+            ref[1] = jnp.zeros(ref.shape[1:], jnp.float32)
+        xsrc[pl.ds(width + 16, 16), :] = jnp.zeros((16, xsrc.shape[1]), xsrc.dtype)
+
+    xsrc[pl.ds(width + 32, 96), :] = jnp.zeros((96, xsrc.shape[1]), xsrc.dtype)
+    pl.semaphore_wait(barrier, ny - 1 + nx - 1)
+
+    def edge_rows(src, lead, dst, lo, n, k, sends, recvs):
+        planes_of = pl.ds(lo, n)
+        down = remote(src.at[planes_of, pl.ds(lead + y_rows - PAD, PAD), :], dst.at[planes_of, pl.ds(0, PAD), :],
+                      sends.at[k, 0], recvs.at[k, 0], gx, lax.rem(gy + 1, ny))
+        up = remote(src.at[planes_of, pl.ds(lead, PAD), :], dst.at[planes_of, pl.ds(PAD + y_rows, PAD), :],
+                    sends.at[k, 1], recvs.at[k, 1], gx, lax.rem(gy + ny - 1, ny))
+        return down, up
+
+    def columns(src, dst, k):
+        right = remote(src.at[0], dst.at[0], col_send.at[k, 0], col_recv.at[k, 0], lax.rem(gx + 1, nx), gy)
+        left = remote(src.at[1], dst.at[1], col_send.at[k, 1], col_recv.at[k, 1], lax.rem(gx + nx - 1, nx), gy)
+        return right, left
+
+    def inverse_rows():
+        right = remote(x_hbm.at[pl.ds(width - 16, 16), :], xsrc.at[pl.ds(width, 16), :],
+                       xr_send.at[0], xr_recv.at[0], lax.rem(gx + 1, nx), gy)
+        left = remote(x_hbm.at[pl.ds(0, 16), :], xsrc.at[pl.ds(width + 16, 16), :],
+                      xr_send.at[1], xr_recv.at[1], lax.rem(gx + nx - 1, nx), gy)
+        return right, left
+
+    def both(pair, ok_after, ok_before, act_after, act_before):
+        @pl.when(ok_after)
+        def _():
+            act_on(pair[0], act_after)
+
+        @pl.when(ok_before)
+        def _():
+            act_on(pair[1], act_before)
+
+    def act_on(copy, act):
+        if act == 0:
+            copy.start()
+        elif act == 1:
+            copy.wait_send()
+        else:
+            copy.wait_recv()
+
+    def start_rows(pair):
+        both(pair, down_ok, up_ok, 0, 0)
+
+    def sent_rows(pair):
+        both(pair, down_ok, up_ok, 1, 1)
+
+    def got_rows(pair):
+        both(pair, up_ok, down_ok, 2, 2)
+
+    def start_cols(pair):
+        both(pair, right_ok, left_ok, 0, 0)
+
+    def sent_cols(pair):
+        both(pair, right_ok, left_ok, 1, 1)
+
+    def got_cols(pair):
+        both(pair, left_ok, right_ok, 2, 2)
+
+    m_rows = edge_rows(mobility, 0, m, 0, planes, 0, row_send, row_recv)
+    v_rows = edge_rows(phase, 0, v, 0, planes, 1, row_send, row_recv)
+    f_rows = edge_rows(f, PAD, f, 0, planes, 2, row_send, row_recv)
+    start_rows(m_rows)
+    start_rows(v_rows)
+    start_cols(inverse_rows())
+
+    def y_own(d):
+        return remote(y_hbm.at[pl.ds(pl.multiple_of(side_half * depth, depth), depth), :], yinv.at[gy, side_half],
+                      y_send.at[0, d], y_recv.at[0, d], gx, lax.rem(gy + 2 * d, ny))
+
+    def y_arrived(d):
+        slot = lax.rem(gy - 2 * d + ny, ny)
+        return remote(yinv.at[slot, side_half], yinv.at[slot, side_half], y_send.at[0, d], y_recv.at[0, d],
+                      gx, lax.rem(gy + 2 * d, ny))
+
+    def y_mate(d):
+        slot = lax.rem(gy - 2 * d + ny, ny)
+        src = y_hbm.at[pl.ds(pl.multiple_of(side_half * depth, depth), depth), :] if d == 0 else yinv.at[slot, side_half]
+        return remote(src, yinv.at[slot, side_half], y_send.at[1, d], y_recv.at[1, d], gx, mate)
+
+    def y_from_mate(d):
+        slot = lax.rem(mate - 2 * d + ny, ny)
+        return remote(yinv.at[slot, side_half], yinv.at[slot, side_half], y_send.at[1, d], y_recv.at[1, d], gx, mate)
+
+    def y_partner(k):
+        slot = lax.rem(gy + k, ny)
+        return remote(yinv.at[slot, side_half], yinv.at[slot, side_half], y_send.at[2, k], y_recv.at[2, k], partner, gy)
+
+    def y_from_partner(k):
+        slot = lax.rem(gy + k, ny)
+        return remote(yinv.at[slot, 1 - side_half], yinv.at[slot, 1 - side_half], y_send.at[2, k], y_recv.at[2, k],
+                      partner, gy)
+
+    for d in range(1, y_half):
+        y_own(d).start()
+    y_mate(0).start()
+
+    for ref in (v, m, f):
+        ref[planes] = jnp.zeros(ref.shape[1:], jnp.float32)
+    above[...] = jnp.zeros_like(above)
+
+    pack_lane = lax.broadcasted_iota(jnp.int32, (y_rows, 128), 1)
+    e1[...] = jnp.zeros_like(e1)
+    e2[...] = jnp.zeros_like(e2)
+    loads[0].wait()
+    loads[1].wait()
+
+    @pl.loop(0, planes)
+    def _(z):
+        for ref, base in ((v, 0), (m, planes)):
+            last = ref[z, pl.ds(PAD, y_rows), pl.ds(width - 128, 128)]
+            lead = ref[z, pl.ds(PAD, y_rows), pl.ds(0, 128)]
+            here = pack_lane == z + base
+            e1[0] = jnp.where(here, last[:, 127:128], e1[0])
+            e1[1] = jnp.where(here, lead[:, 0:1], e1[1])
+
+    v_cols = columns(e1, r1, 0)
+    f_cols = columns(e2, r2, 1)
+    start_cols(v_cols)
+
+    loads[2].wait()
+    got_cols(inverse_rows())
+    for b in range(nx):
+        xt[b] = xsrc[:, b * width:(b + 1) * width].T
+
+    got_rows(m_rows)
+    got_rows(v_rows)
+    got_cols(v_cols)
+
+    strip_lane = lax.broadcasted_iota(jnp.int32, (STRIP, 128), 1)
+
+    def pick(ref, side, mine, at):
+        return jnp.sum(jnp.where(strip_lane == at, ref[side, mine, :], 0.0), axis=1, keepdims=True)
+
+    def plain_value(u):
+        return u
+
+    def chemical(u):
+        return u * u * u - u
+
+    def cols_from(ref):
+        def cols(z, mine):
+            return (pick(ref, 0, mine, z), pick(ref, 1, mine, z),
+                    pick(r1, 0, mine, z + planes), pick(r1, 1, mine, z + planes))
+        return cols
+
+    @pl.loop(0, planes)
+    def _(z):
+        def store(mine, inner, total):
+            value = v[z, inner, :] + 2.0 * step_size * total
+            f[z, inner, :] = value
+            here = strip_lane == z
+            e2[0, mine, :] = jnp.where(here, value[:, width - 1:width], e2[0, mine, :])
+            e2[1, mine, :] = jnp.where(here, value[:, 0:1], e2[1, mine, :])
+
+        sweep_plane(z, v, m, above, cols_from(r1), plain_value, y_rows, width, store)
+
+    start_rows(f_rows)
+    start_cols(f_cols)
+    above[...] = jnp.zeros_like(above)
+
+    def across(s, d):
+        lo, n = stages[s]
+        return remote(second.at[pl.ds(lo, n)], gath.at[gx, pl.ds(lo, n)], gx_send.at[s, d], gx_recv.at[s, d],
+                      lax.rem(gx + 2 * d, nx), gy)
+
+    def arrived(s, d):
+        lo, n = stages[s]
+        slot = lax.rem(gx - 2 * d + nx, nx)
+        return remote(second.at[pl.ds(lo, n)], gath.at[slot, pl.ds(lo, n)], gx_send.at[s, d], gx_recv.at[s, d],
+                      lax.rem(gx + 2 * d, nx), gy)
+
+    def to_pair(s, d):
+        lo, n = stages[s]
+        slot = lax.rem(gx - 2 * d + nx, nx)
+        src = second.at[pl.ds(lo, n)] if d == 0 else gath.at[slot, pl.ds(lo, n)]
+        return remote(src, gath.at[slot, pl.ds(lo, n)], pair_send.at[s, d], pair_recv.at[s, d], partner, gy)
+
+    def from_pair(s, d):
+        lo, n = stages[s]
+        slot = lax.rem(partner - 2 * d + nx, nx)
+        return remote(second.at[pl.ds(lo, n)], gath.at[slot, pl.ds(lo, n)], pair_send.at[s, d], pair_recv.at[s, d],
+                      partner, gy)
+
+    got_rows(f_rows)
+    got_cols(f_cols)
+
+    for s in range(per):
+        lo, n = stages[s]
+
+        @pl.loop(lo, lo + n)
+        def _(z):
+            def store(mine, inner, total):
+                second[z, mine, :] = (f[z, inner, :] + 2.0 * step_size * total).astype(second.dtype)
+
+            sweep_plane(z, f, m, above, cols_from(r2), plain_value, y_rows, width, store)
+
+        for d in range(1, half):
+            across(s, d).start()
+        to_pair(s, 0).start()
+
+    above[...] = jnp.zeros_like(above)
+    for d in range(1, y_half):
+        y_arrived(d).wait_recv()
+        y_mate(d).start()
+
+    def spread(s, d):
+        peer = lax.rem(gy + d, ny)
+        return remote(upd.at[s, peer], yrecv.at[s, gy], a2a_send.at[s, d], a2a_recv.at[s, d], gx, peer)
+
+    def landed(s, d):
+        return remote(upd.at[s, 0], yrecv.at[s, lax.rem(gy - d + ny, ny)], a2a_send.at[s, d], a2a_recv.at[s, d],
+                      gx, lax.rem(gy + d, ny))
+
+    def back(s, d):
+        peer = lax.rem(gy + d, ny)
+        return remote(upd.at[s, peer], out.at[s, gy], ret_send.at[s, d], ret_recv.at[s, d], gx, peer)
+
+    def returned(s, d):
+        return remote(upd.at[s, 0], out.at[s, lax.rem(gy - d + ny, ny)], ret_send.at[s, d], ret_recv.at[s, d],
+                      gx, lax.rem(gy + d, ny))
+
+    def keep_in(s):
+        return pltpu.make_async_copy(upd.at[s, gy], yrecv.at[s, gy], keep_sems.at[0, s])
+
+    def keep_out(s):
+        return pltpu.make_async_copy(upd.at[s, gy], out.at[s, gy], keep_sems.at[1, s])
+
+    def solved_rows(s):
+        lo, n = stages[s]
+        return edge_rows(v, PAD, v, lo, n, s, sol_send, sol_recv)
+
+    def fetch(z, k):
+        slot = lax.rem(z, 2)
+        return pltpu.make_async_copy(gath.at[lax.rem(gx + k, nx), z], gbuf.at[slot, k - 1], g_sems.at[slot, k - 1])
+
+    def edge_cols(z, mine):
+        beyond = f[z, mine, pl.ds(0, 128)]
+        return (chemical(beyond[:, 15:16]), chemical(beyond[:, 16:17]),
+                pick(r1, 0, mine, z + planes), pick(r1, 1, mine, z + planes))
+
+    def solve_x(s):
+        lo, n = stages[s]
+        for d in range(1, half):
+            arrived(s, d).wait_recv()
+            to_pair(s, d).start()
+        for d in range(half):
+            from_pair(s, d).wait_recv()
+        for k in range(1, nx):
+            fetch(lo, k).start()
+
+        @pl.loop(lo, lo + n)
+        def _(z):
+            @pl.when(z + 1 < lo + n)
+            def _():
+                for k in range(1, nx):
+                    fetch(z + 1, k).start()
+
+            total = jnp.dot(second[z], xt[gx], preferred_element_type=jnp.float32)
+            for k in range(1, nx):
+                fetch(z, k).wait()
+                total = total + jnp.dot(
+                    gbuf[lax.rem(z, 2), k - 1], xt[lax.rem(gx + k, nx)], preferred_element_type=jnp.float32)
+            v[z, pl.ds(PAD, y_rows), :] = total[:, :width]
+            f[z, pl.ds(0, y_rows), pl.ds(0, 128)] = total[:, width:]
+
+        start_rows(solved_rows(s))
+        got_rows(solved_rows(s))
+
+        @pl.loop(s * chunk, (s + 1) * chunk)
+        def _(z):
+            def store(mine, inner, total):
+                value = (v[z, inner, :] + 2.0 * step_size * total).astype(upd.dtype)
+                for c in range(cuts):
+                    upd[s, (z - s * chunk) * cuts + c, mine, :] = value[:, c * w:(c + 1) * w]
+
+            sweep_plane(z, v, m, above, edge_cols, chemical, y_rows, width, store)
+
+        keep_in(s).start()
+
+        @pl.loop(1, ny)
+        def _(d):
+            spread(s, d).start()
+
+    def share_inverse():
+        for d in range(y_half):
+            y_from_mate(d).wait_recv()
+        for k in range(1, ny):
+            y_partner(k).start()
+
+    def solve_y(s):
+        if s == 0:
+            loads[3].wait()
+            loads[4].wait()
+            for k in range(1, ny):
+                y_from_partner(k).wait_recv()
+        keep_in(s).wait()
+
+        @pl.loop(1, ny)
+        def _(d):
+            landed(s, d).wait_recv()
+            spread(s, d).wait_send()
+
+        def block(d):
+            peer = lax.rem(gy + d, ny)
+            lines = yrecv[s].reshape(ny * y_rows, w)
+            upd[s, peer] = jnp.dot(
+                yinv[peer].reshape(y_rows, ny * y_rows), lines, preferred_element_type=jnp.float32).astype(upd.dtype)
+
+        @pl.loop(1, ny)
+        def _(d):
+            block(d)
+            back(s, d).start()
+
+        block(0)
+        keep_out(s).start()
+
+    sent_rows(f_rows)
+    for s in range(per):
+        solve_x(s)
+        if s == 0:
+            share_inverse()
+        else:
+            solve_y(s - 1)
+    solve_y(per - 1)
+
+    for pair in (m_rows, v_rows):
+        sent_rows(pair)
+    for pair in (v_cols, f_cols, inverse_rows()):
+        sent_cols(pair)
+    for d in range(1, y_half):
+        y_own(d).wait_send()
+    for d in range(y_half):
+        y_mate(d).wait_send()
+    for k in range(1, ny):
+        y_partner(k).wait_send()
+    for s in range(per):
+        for d in range(1, half):
+            across(s, d).wait_send()
+        for d in range(half):
+            to_pair(s, d).wait_send()
+        sent_rows(solved_rows(s))
+        keep_out(s).wait()
+
+        @pl.loop(1, ny)
+        def _(d):
+            back(s, d).wait_send()
+            returned(s, d).wait_recv()
+
+
+def local(per, phase_field, mobility, x_inverse, y_inverse):
+    planes, y_rows, width = phase_field.shape
+    nx, ny = lax.axis_size("gx"), lax.axis_size("gy")
+    chunk = planes // per
+    w = chunk * width // ny
+    ends = [min((s + 1) * chunk + 1, planes) for s in range(per)]
+    starts = [0] + ends[:-1]
+    stages = [(lo, hi - lo) for lo, hi in zip(starts, ends)]
+    f32, bf16, dma = jnp.float32, jnp.bfloat16, pltpu.SemaphoreType.DMA
+    tall = pltpu.VMEM((planes + 1, y_rows + 2 * PAD, width), f32)
+    edges = pltpu.VMEM((2, y_rows, 128), f32)
+    any_spec = pl.BlockSpec(memory_space=pl.ANY)
+    lines, _ = pl.pallas_call(
+        functools.partial(step_kernel, nx, ny, stages, w),
+        out_shape=(
+            jax.ShapeDtypeStruct((per, ny, y_rows, w), bf16),
+            jax.ShapeDtypeStruct((nx, planes, y_rows, width), bf16),
+        ),
+        in_specs=[any_spec] * 4,
+        out_specs=(any_spec, any_spec),
+        scratch_shapes=[
+            tall, tall, tall,
+            pltpu.VMEM((planes, y_rows, width), bf16),
+            pltpu.VMEM((2, nx - 1, y_rows, width), bf16),
+            pltpu.VMEM((width + 128, nx * width), bf16),
+            pltpu.VMEM((nx, width, width + 128), bf16),
+            pltpu.VMEM((ny, 2, y_rows // 2, ny * y_rows), bf16),
+            pltpu.VMEM((per, ny, y_rows, w), bf16),
+            pltpu.VMEM((per, ny, y_rows, w), bf16),
+            pltpu.VMEM((y_rows, width), f32),
+            edges, edges, edges, edges,
+            dma((5,)), dma((3, 2)), dma((3, 2)), dma((2, 2)), dma((2, 2)), dma((2,)), dma((2,)),
+            dma((3, ny)), dma((3, ny)),
+            dma((per, nx // 2)), dma((per, nx // 2)), dma((per, nx // 2)), dma((per, nx // 2)),
+            dma((per, 2)), dma((per, 2)),
+            dma((per, ny)), dma((per, ny)), dma((per, ny)), dma((per, ny)),
+            dma((2, per)), dma((2, nx - 1)),
+        ],
+        compiler_params=pltpu.CompilerParams(
+            collective_id=0, has_side_effects=True, vmem_limit_bytes=62 * 2**20),
+        cost_estimate=pl.CostEstimate(
+            flops=8400 * phase_field.size, bytes_accessed=40 * phase_field.size, transcendentals=0),
+    )(phase_field, mobility, x_inverse, y_inverse)
+    lines = lines.reshape(planes, width // w, y_rows, w)
+    return jnp.transpose(lines, (0, 2, 1, 3)).reshape(planes, y_rows, width).astype(jnp.float32)
+
+
+def chunks(planes, y_rows, width, nx, ny):
+    if nx % 2 or ny % 2 or nx < 4 or ny < 4 or y_rows % STRIP or width % 128 or planes > 64:
+        return 0
+    if 30 * planes * y_rows * width > 64 * 2**20:
+        return 0
+    for per in (4, 2, 1):
+        if planes % per == 0 and planes // per * width % ny == 0:
+            w = planes // per * width // ny
+            if w % 128 == 0 and width % w == 0:
+                return per
+    return 0
+
+
 def solution(mesh):
     placed = (P(None, "gy", "gx"), P(None, "gy", "gx"), P("gx", None), P("gy", None))
-    return jax.shard_map(
-        local, mesh=mesh, in_specs=placed, out_specs=P(None, "gy", "gx"), check_vma=False
-    )
+    nx, ny = mesh.shape["gx"], mesh.shape["gy"]
+
+    def step(phase_field, mobility, x_inverse, y_inverse):
+        planes, rows, cols = phase_field.shape
+        per = chunks(planes, rows // ny, cols // nx, nx, ny)
+        body = functools.partial(local, per) if per else plain
+        return jax.shard_map(
+            body, mesh=mesh, in_specs=placed, out_specs=P(None, "gy", "gx"), check_vma=False
+        )(phase_field, mobility, x_inverse, y_inverse)
+
+    return step

time: 799 us -> 380 us (0.48)
  Pallas kernels: 0 us -> 366 us
  blocking collectives: 332 us -> 0 us
  other arithmetic: 190 us -> 3.22 us
  waiting for transfers between devices: 126 us -> 0 us
  local copies, waits for them, and re-layouts: 69.5 us -> 4.47 us
  matrix products: 28.8 us -> 0 us
  starting transfers between devices: 28 us -> 0 us
  between operations: 15.4 us -> 0.02 us
    pallas_call x0 -> x1, Pallas kernels: none -> 366 us  [local(): pl.pallas_call(functools.partial(step_kernel, nx, ny, stages, w), out_sha...]
    all_to_all x2 -> x0, blocking collectives: 332 us -> none  [the longest x1 187 us: local(): lax.all_to_all(solved_cols, 'gy', split_axis=0, concat_axis=1, tiled=True)]
    all_gather x2 -> x0, waiting for transfers between devices: 107 us -> none  [the longest x1 107 us: local(): segment = lax.all_gather(second, 'gx', axis=2, tiled=True)]
    concatenate x5 -> x0, other arithmetic: 48.9 us -> none  [extended(): x = jnp.concatenate([before, x, after], axis=dim)]
    convert_element_type x1 -> x0, other arithmetic: 43.8 us -> none  [local(): (first + step_size * laplace(first_pad, mob_near)).astype(jnp.bfloat16)]
    transpose x1 -> x0, other arithmetic: 43.7 us -> none  [local(): columns = jnp.transpose(updated, (1, 0, 2)).reshape(y_rows, planes * x_rows)]
    add x1 -> x0, other arithmetic: 43 us -> none  [local(): first = phase_field + step_size * laplace(padded[0], mob_near)]
    dot_general x2 -> x0, matrix products: 28.8 us -> none  [the longest x1 16.2 us: local(): lax.dot_general(flat, x_inverse, (((1,), (1,)), ((), ())), preferred_elem...]
  transfers between devices with their start and end apart: 14 -> 0, of which waited for: 10 -> 0; matrix products, arithmetic and copies ran while one was open for 10% -> 0% of each run, Pallas kernels for 0% -> 0%
where the time goes in v1:
time: 380 us; the launch traced here: 374 us
  Pallas kernels  366 us (96%)
  local copies, waits for them, and re-layouts  4.47 us (1%)
    pallas_call x1, Pallas kernels, local(): pl.pallas_call(functools.partial(step_kernel, nx, ny, stages, w), out_sha...  366 us

profile of v1, /device:TPU:0, one launch (start us, length us, event | category | flops | bytes accessed | tf_op | source)
XLA Modules:
  0.0 373.6 jit_solution(10022334349199021300)
XLA Ops:
  0.0 365.9 %shard_map.46 = (bf16[4,8,256,256]{3,2,1,0:T(8,128)(2,1)}, bf16[4,16,256,512]{3,2,1,0:T(8,128)(2,1)}) custom-call(f32[16,256,512]{2,1,0:T(8,128)} %phase.1, f32[16,256,512]{2,1,0:T(8,128)} %mobility.1, bf16[512,2048]{1,0:T(8,128)(2,1)} %x_hbm.1, bf16[256,2048]{1,0:T(8,128)(2,1)} %y_hbm.1), custom_call_target="tpu_custom_call" | custom-call | flops 17616076800 | bytes 83886080 | tf_op jit(solution)/shard_map/pallas_call | solution.py:541
  365.9 3.2 convert_bitcast_fusion
  369.1 4.5 %copy.6 = f32[16,2,32,8,256]{4,3,1,2,0:T(8,128)} copy(f32[16,2,32,8,256]{4,3,2,1,0:T(8,128)S(1)} %convert_bitcast_fusion) | data formatting | bytes 16777216 | tf_op jit(solution)/shard_map/convert_element_type | solution.py:573

commit v2 on v1

--- a/solution.py
+++ b/solution.py
@@ -115,8 +115,8 @@
 def step_kernel(
     nx, ny, stages, w,
     phase, mobility, x_hbm, y_hbm, out, gath,
-    v, m, f, second, gbuf, xsrc, xt, yinv, upd, yrecv, above, e1, r1, e2, r2,
-    load_sems, row_send, row_recv, col_send, col_recv, xr_send, xr_recv,
+    v, m, f, second, gbuf, xsrc, xt, yinv, upd, yrecv, above1, above2, above3, e1, r1, e2, r2,
+    load_sems, in_sems, row_send, row_recv, f_send, f_recv, col_send, col_recv, xr_send, xr_recv,
     y_send, y_recv, gx_send, gx_recv, pair_send, pair_recv, sol_send, sol_recv,
     a2a_send, a2a_recv, ret_send, ret_recv, keep_sems, g_sems,
 ):
@@ -143,12 +143,18 @@
         pl.semaphore_signal(barrier, inc=1, device_id=(lax.rem(gx + d, nx), gy), device_id_type=MESH)
 
     loads = [
-        pltpu.make_async_copy(phase, v.at[every, pl.ds(PAD, y_rows), :], load_sems.at[0]),
-        pltpu.make_async_copy(mobility, m.at[every, pl.ds(PAD, y_rows), :], load_sems.at[1]),
-        pltpu.make_async_copy(x_hbm, xsrc.at[pl.ds(0, width), :], load_sems.at[2]),
-        pltpu.make_async_copy(y_hbm.at[pl.ds(0, depth), :], yinv.at[gy, 0], load_sems.at[3]),
-        pltpu.make_async_copy(y_hbm.at[pl.ds(depth, depth), :], yinv.at[gy, 1], load_sems.at[4]),
+        pltpu.make_async_copy(x_hbm, xsrc.at[pl.ds(0, width), :], load_sems.at[0]),
+        pltpu.make_async_copy(y_hbm.at[pl.ds(0, depth), :], yinv.at[gy, 0], load_sems.at[1]),
+        pltpu.make_async_copy(y_hbm.at[pl.ds(depth, depth), :], yinv.at[gy, 1], load_sems.at[2]),
     ]
+    def load(g):
+        group = pl.ds(g * chunk, chunk)
+        return (pltpu.make_async_copy(phase.at[group], v.at[group, pl.ds(PAD, y_rows), :], in_sems.at[g, 0]),
+                pltpu.make_async_copy(mobility.at[group], m.at[group, pl.ds(PAD, y_rows), :], in_sems.at[g, 1]))
+
+    for g in range(per):
+        for copy in load(g):
+            copy.start()
     for copy in loads:
         copy.start()
 
@@ -167,14 +173,16 @@
 
     @pl.when(gx == 0)
     def _():
-        for ref in (r1, r2):
-            ref[0] = jnp.zeros(ref.shape[1:], jnp.float32)
+        r1[0] = jnp.zeros(r1.shape[1:], jnp.float32)
+        for g in range(per):
+            r2[g, 0] = jnp.zeros(r1.shape[1:], jnp.float32)
         xsrc[pl.ds(width, 16), :] = jnp.zeros((16, xsrc.shape[1]), xsrc.dtype)
 
     @pl.when(gx == nx - 1)
     def _():
-        for ref in (r1, r2):
-            ref[1] = jnp.zeros(ref.shape[1:], jnp.float32)
+        r1[1] = jnp.zeros(r1.shape[1:], jnp.float32)
+        for g in range(per):
+            r2[g, 1] = jnp.zeros(r1.shape[1:], jnp.float32)
         xsrc[pl.ds(width + 16, 16), :] = jnp.zeros((16, xsrc.shape[1]), xsrc.dtype)
 
     xsrc[pl.ds(width + 32, 96), :] = jnp.zeros((96, xsrc.shape[1]), xsrc.dtype)
@@ -237,7 +245,6 @@
 
     m_rows = edge_rows(mobility, 0, m, 0, planes, 0, row_send, row_recv)
     v_rows = edge_rows(phase, 0, v, 0, planes, 1, row_send, row_recv)
-    f_rows = edge_rows(f, PAD, f, 0, planes, 2, row_send, row_recv)
     start_rows(m_rows)
     start_rows(v_rows)
     start_cols(inverse_rows())
@@ -269,41 +276,41 @@
         return remote(yinv.at[slot, 1 - side_half], yinv.at[slot, 1 - side_half], y_send.at[2, k], y_recv.at[2, k],
                       partner, gy)
 
+    for ref in (v, m, f):
+        ref[planes] = jnp.zeros(ref.shape[1:], jnp.float32)
+    for ref in (above1, above2, above3):
+        ref[...] = jnp.zeros_like(ref)
+
+    pack_lane = lax.broadcasted_iota(jnp.int32, (y_rows, 128), 1)
+    e1[...] = jnp.zeros_like(e1)
+    e2[...] = jnp.zeros_like(e2)
+    for g in range(per):
+        for copy in load(g):
+            copy.wait()
+
+        @pl.loop(g * chunk, (g + 1) * chunk)
+        def _(z):
+            for ref, base in ((v, 0), (m, planes)):
+                last = ref[z, pl.ds(PAD, y_rows), pl.ds(width - 128, 128)]
+                lead = ref[z, pl.ds(PAD, y_rows), pl.ds(0, 128)]
+                here = pack_lane == z + base
+                e1[0] = jnp.where(here, last[:, 127:128], e1[0])
+                e1[1] = jnp.where(here, lead[:, 0:1], e1[1])
+
+    v_cols = columns(e1, r1, 0)
+    start_cols(v_cols)
+
+    loads[0].wait()
+    got_cols(inverse_rows())
+    for b in range(nx):
+        xt[b] = xsrc[:, b * width:(b + 1) * width].T
+
+    got_rows(m_rows)
+    got_rows(v_rows)
+    got_cols(v_cols)
     for d in range(1, y_half):
         y_own(d).start()
     y_mate(0).start()
-
-    for ref in (v, m, f):
-        ref[planes] = jnp.zeros(ref.shape[1:], jnp.float32)
-    above[...] = jnp.zeros_like(above)
-
-    pack_lane = lax.broadcasted_iota(jnp.int32, (y_rows, 128), 1)
-    e1[...] = jnp.zeros_like(e1)
-    e2[...] = jnp.zeros_like(e2)
-    loads[0].wait()
-    loads[1].wait()
-
-    @pl.loop(0, planes)
-    def _(z):
-        for ref, base in ((v, 0), (m, planes)):
-            last = ref[z, pl.ds(PAD, y_rows), pl.ds(width - 128, 128)]
-            lead = ref[z, pl.ds(PAD, y_rows), pl.ds(0, 128)]
-            here = pack_lane == z + base
-            e1[0] = jnp.where(here, last[:, 127:128], e1[0])
-            e1[1] = jnp.where(here, lead[:, 0:1], e1[1])
-
-    v_cols = columns(e1, r1, 0)
-    f_cols = columns(e2, r2, 1)
-    start_cols(v_cols)
-
-    loads[2].wait()
-    got_cols(inverse_rows())
-    for b in range(nx):
-        xt[b] = xsrc[:, b * width:(b + 1) * width].T
-
-    got_rows(m_rows)
-    got_rows(v_rows)
-    got_cols(v_cols)
 
     strip_lane = lax.broadcasted_iota(jnp.int32, (STRIP, 128), 1)
 
@@ -322,65 +329,75 @@
                     pick(r1, 0, mine, z + planes), pick(r1, 1, mine, z + planes))
         return cols
 
-    @pl.loop(0, planes)
-    def _(z):
-        def store(mine, inner, total):
-            value = v[z, inner, :] + 2.0 * step_size * total
-            f[z, inner, :] = value
-            here = strip_lane == z
-            e2[0, mine, :] = jnp.where(here, value[:, width - 1:width], e2[0, mine, :])
-            e2[1, mine, :] = jnp.where(here, value[:, 0:1], e2[1, mine, :])
-
-        sweep_plane(z, v, m, above, cols_from(r1), plain_value, y_rows, width, store)
-
-    start_rows(f_rows)
-    start_cols(f_cols)
-    above[...] = jnp.zeros_like(above)
-
-    def across(s, d):
-        lo, n = stages[s]
-        return remote(second.at[pl.ds(lo, n)], gath.at[gx, pl.ds(lo, n)], gx_send.at[s, d], gx_recv.at[s, d],
-                      lax.rem(gx + 2 * d, nx), gy)
-
-    def arrived(s, d):
-        lo, n = stages[s]
-        slot = lax.rem(gx - 2 * d + nx, nx)
-        return remote(second.at[pl.ds(lo, n)], gath.at[slot, pl.ds(lo, n)], gx_send.at[s, d], gx_recv.at[s, d],
-                      lax.rem(gx + 2 * d, nx), gy)
-
-    def to_pair(s, d):
-        lo, n = stages[s]
-        slot = lax.rem(gx - 2 * d + nx, nx)
-        src = second.at[pl.ds(lo, n)] if d == 0 else gath.at[slot, pl.ds(lo, n)]
-        return remote(src, gath.at[slot, pl.ds(lo, n)], pair_send.at[s, d], pair_recv.at[s, d], partner, gy)
-
-    def from_pair(s, d):
-        lo, n = stages[s]
-        slot = lax.rem(partner - 2 * d + nx, nx)
-        return remote(second.at[pl.ds(lo, n)], gath.at[slot, pl.ds(lo, n)], pair_send.at[s, d], pair_recv.at[s, d],
-                      partner, gy)
-
-    got_rows(f_rows)
-    got_cols(f_cols)
-
-    for s in range(per):
-        lo, n = stages[s]
+    def f_rows(s):
+        lo, n = stages[s]
+        return edge_rows(f, PAD, f, lo, n, s, f_send, f_recv)
+
+    def f_cols(s):
+        return columns(e2.at[s], r2.at[s], 1 + s)
+
+    def make_first(s):
+        lo, n = stages[s]
+        beyond = lo + n
+
+        @pl.loop(lo + (1 if s else 0), min(beyond + 1, planes))
+        def _(z):
+            def store(mine, inner, total):
+                value = v[z, inner, :] + 2.0 * step_size * total
+                f[z, inner, :] = value
+                here = strip_lane == z
+                t = s if beyond == planes else s + lax.div(z, beyond)
+                e2[t, 0, mine, :] = jnp.where(here, value[:, width - 1:width], e2[t, 0, mine, :])
+                e2[t, 1, mine, :] = jnp.where(here, value[:, 0:1], e2[t, 1, mine, :])
+
+            sweep_plane(z, v, m, above1, cols_from(r1), plain_value, y_rows, width, store)
+
+        start_rows(f_rows(s))
+        start_cols(f_cols(s))
+
+    def make_second(s):
+        lo, n = stages[s]
+        got_rows(f_rows(s))
+        got_cols(f_cols(s))
 
         @pl.loop(lo, lo + n)
         def _(z):
             def store(mine, inner, total):
                 second[z, mine, :] = (f[z, inner, :] + 2.0 * step_size * total).astype(second.dtype)
 
-            sweep_plane(z, f, m, above, cols_from(r2), plain_value, y_rows, width, store)
-
+            sweep_plane(z, f, m, above2, cols_from(r2.at[s]), plain_value, y_rows, width, store)
+
+    def across(s, d):
+        lo, n = stages[s]
+        return remote(second.at[pl.ds(lo, n)], gath.at[gx, pl.ds(lo, n)], gx_send.at[s, d], gx_recv.at[s, d],
+                      lax.rem(gx + 2 * d, nx), gy)
+
+    def arrived(s, d):
+        lo, n = stages[s]
+        slot = lax.rem(gx - 2 * d + nx, nx)
+        return remote(second.at[pl.ds(lo, n)], gath.at[slot, pl.ds(lo, n)], gx_send.at[s, d], gx_recv.at[s, d],
+                      lax.rem(gx + 2 * d, nx), gy)
+
+    def to_pair(s, d):
+        lo, n = stages[s]
+        slot = lax.rem(gx - 2 * d + nx, nx)
+        src = second.at[pl.ds(lo, n)] if d == 0 else gath.at[slot, pl.ds(lo, n)]
+        return remote(src, gath.at[slot, pl.ds(lo, n)], pair_send.at[s, d], pair_recv.at[s, d], partner, gy)
+
+    def from_pair(s, d):
+        lo, n = stages[s]
+        slot = lax.rem(partner - 2 * d + nx, nx)
+        return remote(second.at[pl.ds(lo, n)], gath.at[slot, pl.ds(lo, n)], pair_send.at[s, d], pair_recv.at[s, d],
+                      partner, gy)
+
+    def send_second(s):
         for d in range(1, half):
             across(s, d).start()
         to_pair(s, 0).start()
 
-    above[...] = jnp.zeros_like(above)
-    for d in range(1, y_half):
-        y_arrived(d).wait_recv()
-        y_mate(d).start()
+    def home(s, owner):
+        off = pl.multiple_of(lax.rem(owner, cuts) * w, w)
+        return out.at[s * chunk + lax.div(owner, cuts), :, pl.ds(off, w)]
 
     def spread(s, d):
         peer = lax.rem(gy + d, ny)
@@ -392,17 +409,17 @@
 
     def back(s, d):
         peer = lax.rem(gy + d, ny)
-        return remote(upd.at[s, peer], out.at[s, gy], ret_send.at[s, d], ret_recv.at[s, d], gx, peer)
+        return remote(upd.at[s, peer], home(s, gy), ret_send.at[s, d], ret_recv.at[s, d], gx, peer)
 
     def returned(s, d):
-        return remote(upd.at[s, 0], out.at[s, lax.rem(gy - d + ny, ny)], ret_send.at[s, d], ret_recv.at[s, d],
+        return remote(upd.at[s, 0], home(s, lax.rem(gy - d + ny, ny)), ret_send.at[s, d], ret_recv.at[s, d],
                       gx, lax.rem(gy + d, ny))
 
     def keep_in(s):
         return pltpu.make_async_copy(upd.at[s, gy], yrecv.at[s, gy], keep_sems.at[0, s])
 
     def keep_out(s):
-        return pltpu.make_async_copy(upd.at[s, gy], out.at[s, gy], keep_sems.at[1, s])
+        return pltpu.make_async_copy(upd.at[s, gy], home(s, gy), keep_sems.at[1, s])
 
     def solved_rows(s):
         lo, n = stages[s]
@@ -422,6 +439,13 @@
         for d in range(1, half):
             arrived(s, d).wait_recv()
             to_pair(s, d).start()
+        if s + 1 < per:
+            send_second(s + 1)
+        if s == 0:
+            for d in range(1, y_half):
+                y_arrived(d).wait_recv()
+                y_mate(d).start()
+        sent_rows(f_rows(s))
         for d in range(half):
             from_pair(s, d).wait_recv()
         for k in range(1, nx):
@@ -452,7 +476,7 @@
                 for c in range(cuts):
                     upd[s, (z - s * chunk) * cuts + c, mine, :] = value[:, c * w:(c + 1) * w]
 
-            sweep_plane(z, v, m, above, edge_cols, chemical, y_rows, width, store)
+            sweep_plane(z, v, m, above3, edge_cols, chemical, y_rows, width, store)
 
         keep_in(s).start()
 
@@ -468,8 +492,8 @@
 
     def solve_y(s):
         if s == 0:
-            loads[3].wait()
-            loads[4].wait()
+            loads[1].wait()
+            loads[2].wait()
             for k in range(1, ny):
                 y_from_partner(k).wait_recv()
         keep_in(s).wait()
@@ -493,18 +517,23 @@
         block(0)
         keep_out(s).start()
 
-    sent_rows(f_rows)
+    make_first(0)
+    make_second(0)
+    send_second(0)
     for s in range(per):
+        if s + 1 < per:
+            make_first(s + 1)
+            make_second(s + 1)
         solve_x(s)
-        if s == 0:
+        if s == 1:
             share_inverse()
-        else:
+        if s > 0:
             solve_y(s - 1)
     solve_y(per - 1)
 
     for pair in (m_rows, v_rows):
         sent_rows(pair)
-    for pair in (v_cols, f_cols, inverse_rows()):
+    for pair in [v_cols, inverse_rows()] + [f_cols(s) for s in range(per)]:
         sent_cols(pair)
     for d in range(1, y_half):
         y_own(d).wait_send()
@@ -537,11 +566,13 @@
     f32, bf16, dma = jnp.float32, jnp.bfloat16, pltpu.SemaphoreType.DMA
     tall = pltpu.VMEM((planes + 1, y_rows + 2 * PAD, width), f32)
     edges = pltpu.VMEM((2, y_rows, 128), f32)
+    staged_edges = pltpu.VMEM((per, 2, y_rows, 128), f32)
+    above = pltpu.VMEM((y_rows, width), f32)
     any_spec = pl.BlockSpec(memory_space=pl.ANY)
     lines, _ = pl.pallas_call(
         functools.partial(step_kernel, nx, ny, stages, w),
         out_shape=(
-            jax.ShapeDtypeStruct((per, ny, y_rows, w), bf16),
+            jax.ShapeDtypeStruct((planes, y_rows, width), bf16),
             jax.ShapeDtypeStruct((nx, planes, y_rows, width), bf16),
         ),
         in_specs=[any_spec] * 4,
@@ -555,9 +586,10 @@
             pltpu.VMEM((ny, 2, y_rows // 2, ny * y_rows), bf16),
             pltpu.VMEM((per, ny, y_rows, w), bf16),
             pltpu.VMEM((per, ny, y_rows, w), bf16),
-            pltpu.VMEM((y_rows, width), f32),
-            edges, edges, edges, edges,
-            dma((5,)), dma((3, 2)), dma((3, 2)), dma((2, 2)), dma((2, 2)), dma((2,)), dma((2,)),
+            above, above, above,
+            edges, edges, staged_edges, staged_edges,
+            dma((3,)), dma((per, 2)), dma((2, 2)), dma((2, 2)), dma((per, 2)), dma((per, 2)),
+            dma((1 + per, 2)), dma((1 + per, 2)), dma((2,)), dma((2,)),
             dma((3, ny)), dma((3, ny)),
             dma((per, nx // 2)), dma((per, nx // 2)), dma((per, nx // 2)), dma((per, nx // 2)),
             dma((per, 2)), dma((per, 2)),
@@ -569,8 +601,7 @@
         cost_estimate=pl.CostEstimate(
             flops=8400 * phase_field.size, bytes_accessed=40 * phase_field.size, transcendentals=0),
     )(phase_field, mobility, x_inverse, y_inverse)
-    lines = lines.reshape(planes, width // w, y_rows, w)
-    return jnp.transpose(lines, (0, 2, 1, 3)).reshape(planes, y_rows, width).astype(jnp.float32)
+    return lines.astype(jnp.float32)
 
 
 def chunks(planes, y_rows, width, nx, ny):
@@ -578,7 +609,7 @@
         return 0
     if 30 * planes * y_rows * width > 64 * 2**20:
         return 0
-    for per in (4, 2, 1):
+    for per in (4, 2):
         if planes % per == 0 and planes // per * width % ny == 0:
             w = planes // per * width // ny
             if w % 128 == 0 and width % w == 0:

time: 380 us -> 424 us (1.12)
  Pallas kernels: 366 us -> 410 us
  local copies, waits for them, and re-layouts: 4.47 us -> 0 us
    pallas_call x1, Pallas kernels: 366 us -> 410 us  [local(): pl.pallas_call(functools.partial(step_kernel, nx, ny, stages, w), out_sha...]
    convert_element_type x0 -> x1, other arithmetic: none -> 6.74 us  [local(): return lines.astype(jnp.float32)]
    convert_element_type x1 -> x0, local copies, waits for them, and re-layouts: 4.47 us -> none  [local(): jnp.transpose(lines, (0, 2, 1, 3)).reshape(planes, y_rows, width)]
where the time goes in v2:
time: 424 us; the launch traced here: 417 us
  Pallas kernels  410 us (97%)
  other arithmetic  6.74 us (2%)
    pallas_call x1, Pallas kernels, local(): pl.pallas_call(functools.partial(step_kernel, nx, ny, stages, w), out_sha...  410 us

profile of v2, /device:TPU:0, one launch (start us, length us, event | category | flops | bytes accessed | tf_op | source)
XLA Modules:
  0.0 416.5 jit_solution(5932999878725898239)
XLA Ops:
  0.0 409.8 %shard_map.46 = (bf16[16,256,512]{2,1,0:T(8,128)(2,1)}, bf16[4,16,256,512]{3,2,1,0:T(8,128)(2,1)}) custom-call(f32[16,256,512]{2,1,0:T(8,128)} %phase.1, f32[16,256,512]{2,1,0:T(8,128)} %mobility.1, bf16[512,2048]{1,0:T(8,128)(2,1)} %x_hbm.1, bf16[256,2048]{1,0:T(8,128)(2,1)} %y_hbm.1), custom_call_target="tpu_custom_call" | custom-call | flops 17616076800 | bytes 83886080 | tf_op jit(solution)/shard_map/pallas_call | solution.py:572
  409.8 6.7 %convert_element_type.3 = f32[16,256,512]{2,1,0:T(8,128)} convert(bf16[16,256,512]{2,1,0:T(8,128)(2,1)} %get-tuple-element.6) | non-fusion elementwise | flops 2097152 | bytes 12582912 | tf_op jit(solution)/shard_map/convert_element_type | solution.py:604

commit v3 on v2

--- a/solution.py
+++ b/solution.py
@@ -366,34 +366,34 @@
                 second[z, mine, :] = (f[z, inner, :] + 2.0 * step_size * total).astype(second.dtype)
 
             sweep_plane(z, f, m, above2, cols_from(r2.at[s]), plain_value, y_rows, width, store)
-
-    def across(s, d):
+            for d in range(1, half):
+                across(z, d).start()
+            to_pair(z, 0).start()
+
+    def across(z, d):
+        return remote(second.at[z], gath.at[gx, z], gx_send.at[z, d], gx_recv.at[z, d], lax.rem(gx + 2 * d, nx), gy)
+
+    def arrived(z, d):
+        slot = lax.rem(gx - 2 * d + nx, nx)
+        return remote(second.at[z], gath.at[slot, z], gx_send.at[z, d], gx_recv.at[z, d], lax.rem(gx + 2 * d, nx), gy)
+
+    def to_pair(z, d):
+        slot = lax.rem(gx - 2 * d + nx, nx)
+        src = second.at[z] if d == 0 else gath.at[slot, z]
+        return remote(src, gath.at[slot, z], pair_send.at[z, d], pair_recv.at[z, d], partner, gy)
+
+    def from_pair(z, d):
+        slot = lax.rem(partner - 2 * d + nx, nx)
+        return remote(second.at[z], gath.at[slot, z], pair_send.at[z, d], pair_recv.at[z, d], partner, gy)
+
+    def forward(s):
         lo, n = stages[s]
-        return remote(second.at[pl.ds(lo, n)], gath.at[gx, pl.ds(lo, n)], gx_send.at[s, d], gx_recv.at[s, d],
-                      lax.rem(gx + 2 * d, nx), gy)
-
-    def arrived(s, d):
-        lo, n = stages[s]
-        slot = lax.rem(gx - 2 * d + nx, nx)
-        return remote(second.at[pl.ds(lo, n)], gath.at[slot, pl.ds(lo, n)], gx_send.at[s, d], gx_recv.at[s, d],
-                      lax.rem(gx + 2 * d, nx), gy)
-
-    def to_pair(s, d):
-        lo, n = stages[s]
-        slot = lax.rem(gx - 2 * d + nx, nx)
-        src = second.at[pl.ds(lo, n)] if d == 0 else gath.at[slot, pl.ds(lo, n)]
-        return remote(src, gath.at[slot, pl.ds(lo, n)], pair_send.at[s, d], pair_recv.at[s, d], partner, gy)
-
-    def from_pair(s, d):
-        lo, n = stages[s]
-        slot = lax.rem(partner - 2 * d + nx, nx)
-        return remote(second.at[pl.ds(lo, n)], gath.at[slot, pl.ds(lo, n)], pair_send.at[s, d], pair_recv.at[s, d],
-                      partner, gy)
-
-    def send_second(s):
-        for d in range(1, half):
-            across(s, d).start()
-        to_pair(s, 0).start()
+
+        @pl.loop(lo, lo + n)
+        def _(z):
+            for d in range(1, half):
+                arrived(z, d).wait_recv()
+                to_pair(z, d).start()
 
     def home(s, owner):
         off = pl.multiple_of(lax.rem(owner, cuts) * w, w)
@@ -436,18 +436,13 @@
 
     def solve_x(s):
         lo, n = stages[s]
-        for d in range(1, half):
-            arrived(s, d).wait_recv()
-            to_pair(s, d).start()
-        if s + 1 < per:
-            send_second(s + 1)
-        if s == 0:
-            for d in range(1, y_half):
-                y_arrived(d).wait_recv()
-                y_mate(d).start()
         sent_rows(f_rows(s))
-        for d in range(half):
-            from_pair(s, d).wait_recv()
+
+        @pl.loop(lo, lo + n)
+        def _(z):
+            for d in range(half):
+                from_pair(z, d).wait_recv()
+
         for k in range(1, nx):
             fetch(lo, k).start()
 
@@ -517,14 +512,19 @@
         block(0)
         keep_out(s).start()
 
-    make_first(0)
-    make_second(0)
-    send_second(0)
     for s in range(per):
+        make_first(s)
+        make_second(s)
+        if s == per - 2:
+            forward(0)
+            for d in range(1, y_half):
+                y_arrived(d).wait_recv()
+                y_mate(d).start()
+
+    for s in range(per):
+        solve_x(s)
         if s + 1 < per:
-            make_first(s + 1)
-            make_second(s + 1)
-        solve_x(s)
+            forward(s + 1)
         if s == 1:
             share_inverse()
         if s > 0:
@@ -541,11 +541,14 @@
         y_mate(d).wait_send()
     for k in range(1, ny):
         y_partner(k).wait_send()
+    @pl.loop(0, planes)
+    def _(z):
+        for d in range(1, half):
+            across(z, d).wait_send()
+        for d in range(half):
+            to_pair(z, d).wait_send()
+
     for s in range(per):
-        for d in range(1, half):
-            across(s, d).wait_send()
-        for d in range(half):
-            to_pair(s, d).wait_send()
         sent_rows(solved_rows(s))
         keep_out(s).wait()
 
@@ -591,7 +594,7 @@
             dma((3,)), dma((per, 2)), dma((2, 2)), dma((2, 2)), dma((per, 2)), dma((per, 2)),
             dma((1 + per, 2)), dma((1 + per, 2)), dma((2,)), dma((2,)),
             dma((3, ny)), dma((3, ny)),
-            dma((per, nx // 2)), dma((per, nx // 2)), dma((per, nx // 2)), dma((per, nx // 2)),
+            dma((planes, nx // 2)), dma((planes, nx // 2)), dma((planes, nx // 2)), dma((planes, nx // 2)),
             dma((per, 2)), dma((per, 2)),
             dma((per, ny)), dma((per, ny)), dma((per, ny)), dma((per, ny)),
             dma((2, per)), dma((2, nx - 1)),

time: 424 us -> 426 us (level)
  no operation moved by 1% of the time
where the time goes in v3:
time: 426 us; the launch traced here: 419 us
  Pallas kernels  413 us (97%)
  other arithmetic  6.74 us (2%)
    pallas_call x1, Pallas kernels, local(): pl.pallas_call(functools.partial(step_kernel, nx, ny, stages, w), out_sha...  413 us

profile of v3, /device:TPU:0, one launch (start us, length us, event | category | flops | bytes accessed | tf_op | source)
XLA Modules:
  0.0 419.4 jit_solution(4043950259845926500)
XLA Ops:
  0.0 412.6 %shard_map.46 = (bf16[16,256,512]{2,1,0:T(8,128)(2,1)}, bf16[4,16,256,512]{3,2,1,0:T(8,128)(2,1)}) custom-call(f32[16,256,512]{2,1,0:T(8,128)} %phase.1, f32[16,256,512]{2,1,0:T(8,128)} %mobility.1, bf16[512,2048]{1,0:T(8,128)(2,1)} %x_hbm.1, bf16[256,2048]{1,0:T(8,128)(2,1)} %y_hbm.1), custom_call_target="tpu_custom_call" | custom-call | flops 17616076800 | bytes 83886080 | tf_op jit(solution)/shard_map/pallas_call | solution.py:575
  412.6 6.7 %convert_element_type.3 = f32[16,256,512]{2,1,0:T(8,128)} convert(bf16[16,256,512]{2,1,0:T(8,128)(2,1)} %get-tuple-element.6) | non-fusion elementwise | flops 2097152 | bytes 12582912 | tf_op jit(solution)/shard_map/convert_element_type | solution.py:607

commit v4 on v1

--- a/solution.py
+++ b/solution.py
@@ -10,6 +10,7 @@
 step_size = 0.15
 PAD = 8
 STRIP = 32
+LONG = 16
 MESH = pl.DeviceIdType.MESH
 
 
@@ -82,22 +83,22 @@
     return center_mob * near_mob * inverse
 
 
-def sweep_plane(z, v, m, above, cols, chemical, y_rows, width, store):
+def sweep_plane(z, v, m, above, cols, chemical, base, rows, n, width, store):
     def flux_down(r, n):
         tall_v, tall_m = chemical(v[z, pl.ds(r, n + PAD), :]), m[z, pl.ds(r, n + PAD), :]
         low_v, low_m = pltpu.roll(tall_v, n + PAD - 1, 0)[:n], pltpu.roll(tall_m, n + PAD - 1, 0)[:n]
         return half_mob(tall_m[:n], low_m) * (low_v - tall_v[:n]), tall_v[:n], tall_m[:n]
 
     def strip(i, carried):
-        r = pl.multiple_of(i * STRIP, STRIP)
-        inner, mine = pl.ds(r + PAD, STRIP), pl.ds(r, STRIP)
-        down, own, mob = flux_down(r + PAD, STRIP)
+        r = pl.multiple_of(i * n + base, PAD)
+        inner = pl.ds(r, n)
+        down, own, mob = flux_down(r, n)
         stacked = jnp.concatenate([carried, down], axis=0)
         total = down - pltpu.roll(stacked, 1, 0)[PAD:]
         below = half_mob(mob, m[z + 1, inner, :]) * (chemical(v[z + 1, inner, :]) - own)
-        total = total + (below - above[mine, :])
-        above[mine, :] = below
-        v_left, v_right, m_left, m_right = cols(z, mine)
+        total = total + (below - above[inner, :])
+        above[inner, :] = below
+        v_left, v_right, m_left, m_right = cols(z, inner)
         lane = lax.broadcasted_iota(jnp.int32, own.shape, 1)
         at_end = lane == width - 1
         v_next = jnp.where(at_end, v_right, pltpu.roll(own, width - 1, 1))
@@ -105,11 +106,11 @@
         flux = half_mob(mob, m_next) * (v_next - own)
         entering = half_mob(m_left, mob[:, 0:1]) * (own[:, 0:1] - v_left)
         total = total + (flux - jnp.where(lane == 0, entering, pltpu.roll(flux, 1, 1)))
-        store(mine, inner, total)
-        return down[STRIP - PAD:]
-
-    first_carry, _, _ = flux_down(0, PAD)
-    lax.fori_loop(0, y_rows // STRIP, strip, first_carry)
+        store(inner, pl.ds(pl.multiple_of(i * n, n), n), total)
+        return down[n - PAD:]
+
+    carry = flux_down(base - PAD, PAD)[0] if base else jnp.zeros((PAD, width), jnp.float32)
+    lax.fori_loop(0, rows // n, strip, carry)
 
 
 def step_kernel(
@@ -117,7 +118,7 @@
     phase, mobility, x_hbm, y_hbm, out, gath,
     v, m, f, second, gbuf, xsrc, xt, yinv, upd, yrecv, above, e1, r1, e2, r2,
     load_sems, row_send, row_recv, col_send, col_recv, xr_send, xr_recv,
-    y_send, y_recv, gx_send, gx_recv, pair_send, pair_recv, sol_send, sol_recv,
+    y_send, y_recv, gx_send, gx_recv, pair_send, pair_recv,
     a2a_send, a2a_recv, ret_send, ret_recv, keep_sems, g_sems,
 ):
     planes, y_rows, width = phase.shape
@@ -131,6 +132,7 @@
     cuts = width // w
     depth = y_rows // 2
     every = pl.ds(0, planes)
+    tall = y_rows + 2 * PAD
 
     def remote(src, dst, send, recv, x_to, y_to):
         return pltpu.make_async_remote_copy(
@@ -237,7 +239,6 @@
 
     m_rows = edge_rows(mobility, 0, m, 0, planes, 0, row_send, row_recv)
     v_rows = edge_rows(phase, 0, v, 0, planes, 1, row_send, row_recv)
-    f_rows = edge_rows(f, PAD, f, 0, planes, 2, row_send, row_recv)
     start_rows(m_rows)
     start_rows(v_rows)
     start_cols(inverse_rows())
@@ -269,25 +270,27 @@
         return remote(yinv.at[slot, 1 - side_half], yinv.at[slot, 1 - side_half], y_send.at[2, k], y_recv.at[2, k],
                       partner, gy)
 
-    for d in range(1, y_half):
-        y_own(d).start()
-    y_mate(0).start()
-
     for ref in (v, m, f):
         ref[planes] = jnp.zeros(ref.shape[1:], jnp.float32)
+        ref[every, pl.ds(tall, PAD), :] = jnp.zeros((planes, PAD, width), jnp.float32)
     above[...] = jnp.zeros_like(above)
 
-    pack_lane = lax.broadcasted_iota(jnp.int32, (y_rows, 128), 1)
+    pack_lane = lax.broadcasted_iota(jnp.int32, (tall, 128), 1)
     e1[...] = jnp.zeros_like(e1)
     e2[...] = jnp.zeros_like(e2)
     loads[0].wait()
     loads[1].wait()
+    got_rows(m_rows)
+    got_rows(v_rows)
+    for d in range(1, y_half):
+        y_own(d).start()
+    y_mate(0).start()
 
     @pl.loop(0, planes)
     def _(z):
         for ref, base in ((v, 0), (m, planes)):
-            last = ref[z, pl.ds(PAD, y_rows), pl.ds(width - 128, 128)]
-            lead = ref[z, pl.ds(PAD, y_rows), pl.ds(0, 128)]
+            last = ref[z, pl.ds(0, tall), pl.ds(width - 128, 128)]
+            lead = ref[z, pl.ds(0, tall), pl.ds(0, 128)]
             here = pack_lane == z + base
             e1[0] = jnp.where(here, last[:, 127:128], e1[0])
             e1[1] = jnp.where(here, lead[:, 0:1], e1[1])
@@ -301,14 +304,12 @@
     for b in range(nx):
         xt[b] = xsrc[:, b * width:(b + 1) * width].T
 
-    got_rows(m_rows)
-    got_rows(v_rows)
     got_cols(v_cols)
 
-    strip_lane = lax.broadcasted_iota(jnp.int32, (STRIP, 128), 1)
-
     def pick(ref, side, mine, at):
-        return jnp.sum(jnp.where(strip_lane == at, ref[side, mine, :], 0.0), axis=1, keepdims=True)
+        packed = ref[side, mine, :]
+        lane = lax.broadcasted_iota(jnp.int32, packed.shape, 1)
+        return jnp.sum(jnp.where(lane == at, packed, 0.0), axis=1, keepdims=True)
 
     def plain_value(u):
         return u
@@ -324,16 +325,15 @@
 
     @pl.loop(0, planes)
     def _(z):
-        def store(mine, inner, total):
-            value = v[z, inner, :] + 2.0 * step_size * total
-            f[z, inner, :] = value
-            here = strip_lane == z
+        def store(mine, _, total):
+            value = v[z, mine, :] + 2.0 * step_size * total
+            f[z, mine, :] = value
+            here = lax.broadcasted_iota(jnp.int32, (mine.size, 128), 1) == z
             e2[0, mine, :] = jnp.where(here, value[:, width - 1:width], e2[0, mine, :])
             e2[1, mine, :] = jnp.where(here, value[:, 0:1], e2[1, mine, :])
 
-        sweep_plane(z, v, m, above, cols_from(r1), plain_value, y_rows, width, store)
-
-    start_rows(f_rows)
+        sweep_plane(z, v, m, above, cols_from(r1), plain_value, 0, tall, LONG, width, store)
+
     start_cols(f_cols)
     above[...] = jnp.zeros_like(above)
 
@@ -360,7 +360,6 @@
         return remote(second.at[pl.ds(lo, n)], gath.at[slot, pl.ds(lo, n)], pair_send.at[s, d], pair_recv.at[s, d],
                       partner, gy)
 
-    got_rows(f_rows)
     got_cols(f_cols)
 
     for s in range(per):
@@ -368,10 +367,10 @@
 
         @pl.loop(lo, lo + n)
         def _(z):
-            def store(mine, inner, total):
-                second[z, mine, :] = (f[z, inner, :] + 2.0 * step_size * total).astype(second.dtype)
-
-            sweep_plane(z, f, m, above, cols_from(r2), plain_value, y_rows, width, store)
+            def store(mine, _, total):
+                second[z, mine, :] = (f[z, mine, :] + 2.0 * step_size * total).astype(second.dtype)
+
+            sweep_plane(z, f, m, above, cols_from(r2), plain_value, 0, tall, LONG, width, store)
 
         for d in range(1, half):
             across(s, d).start()
@@ -403,10 +402,6 @@
 
     def keep_out(s):
         return pltpu.make_async_copy(upd.at[s, gy], out.at[s, gy], keep_sems.at[1, s])
-
-    def solved_rows(s):
-        lo, n = stages[s]
-        return edge_rows(v, PAD, v, lo, n, s, sol_send, sol_recv)
 
     def fetch(z, k):
         slot = lax.rem(z, 2)
@@ -439,20 +434,18 @@
                 fetch(z, k).wait()
                 total = total + jnp.dot(
                     gbuf[lax.rem(z, 2), k - 1], xt[lax.rem(gx + k, nx)], preferred_element_type=jnp.float32)
-            v[z, pl.ds(PAD, y_rows), :] = total[:, :width]
-            f[z, pl.ds(0, y_rows), pl.ds(0, 128)] = total[:, width:]
-
-        start_rows(solved_rows(s))
-        got_rows(solved_rows(s))
+            v[z, pl.ds(0, tall), :] = total[:, :width]
+            f[z, pl.ds(0, tall), pl.ds(0, 128)] = total[:, width:]
+
 
         @pl.loop(s * chunk, (s + 1) * chunk)
         def _(z):
-            def store(mine, inner, total):
+            def store(inner, mine, total):
                 value = (v[z, inner, :] + 2.0 * step_size * total).astype(upd.dtype)
                 for c in range(cuts):
                     upd[s, (z - s * chunk) * cuts + c, mine, :] = value[:, c * w:(c + 1) * w]
 
-            sweep_plane(z, v, m, above, edge_cols, chemical, y_rows, width, store)
+            sweep_plane(z, v, m, above, edge_cols, chemical, PAD, y_rows, STRIP, width, store)
 
         keep_in(s).start()
 
@@ -493,7 +486,6 @@
         block(0)
         keep_out(s).start()
 
-    sent_rows(f_rows)
     for s in range(per):
         solve_x(s)
         if s == 0:
@@ -517,7 +509,6 @@
             across(s, d).wait_send()
         for d in range(half):
             to_pair(s, d).wait_send()
-        sent_rows(solved_rows(s))
         keep_out(s).wait()
 
         @pl.loop(1, ny)
@@ -535,32 +526,32 @@
     starts = [0] + ends[:-1]
     stages = [(lo, hi - lo) for lo, hi in zip(starts, ends)]
     f32, bf16, dma = jnp.float32, jnp.bfloat16, pltpu.SemaphoreType.DMA
-    tall = pltpu.VMEM((planes + 1, y_rows + 2 * PAD, width), f32)
-    edges = pltpu.VMEM((2, y_rows, 128), f32)
+    rows = y_rows + 2 * PAD
+    tall = pltpu.VMEM((planes + 1, rows + PAD, width), f32)
+    edges = pltpu.VMEM((2, rows, 128), f32)
     any_spec = pl.BlockSpec(memory_space=pl.ANY)
     lines, _ = pl.pallas_call(
         functools.partial(step_kernel, nx, ny, stages, w),
         out_shape=(
             jax.ShapeDtypeStruct((per, ny, y_rows, w), bf16),
-            jax.ShapeDtypeStruct((nx, planes, y_rows, width), bf16),
+            jax.ShapeDtypeStruct((nx, planes, rows, width), bf16),
         ),
         in_specs=[any_spec] * 4,
         out_specs=(any_spec, any_spec),
         scratch_shapes=[
             tall, tall, tall,
-            pltpu.VMEM((planes, y_rows, width), bf16),
-            pltpu.VMEM((2, nx - 1, y_rows, width), bf16),
+            pltpu.VMEM((planes, rows, width), bf16),
+            pltpu.VMEM((2, nx - 1, rows, width), bf16),
             pltpu.VMEM((width + 128, nx * width), bf16),
             pltpu.VMEM((nx, width, width + 128), bf16),
             pltpu.VMEM((ny, 2, y_rows // 2, ny * y_rows), bf16),
             pltpu.VMEM((per, ny, y_rows, w), bf16),
             pltpu.VMEM((per, ny, y_rows, w), bf16),
-            pltpu.VMEM((y_rows, width), f32),
+            pltpu.VMEM((rows, width), f32),
             edges, edges, edges, edges,
-            dma((5,)), dma((3, 2)), dma((3, 2)), dma((2, 2)), dma((2, 2)), dma((2,)), dma((2,)),
+            dma((5,)), dma((2, 2)), dma((2, 2)), dma((2, 2)), dma((2, 2)), dma((2,)), dma((2,)),
             dma((3, ny)), dma((3, ny)),
             dma((per, nx // 2)), dma((per, nx // 2)), dma((per, nx // 2)), dma((per, nx // 2)),
-            dma((per, 2)), dma((per, 2)),
             dma((per, ny)), dma((per, ny)), dma((per, ny)), dma((per, ny)),
             dma((2, per)), dma((2, nx - 1)),
         ],
@@ -574,7 +565,7 @@
 
 
 def chunks(planes, y_rows, width, nx, ny):
-    if nx % 2 or ny % 2 or nx < 4 or ny < 4 or y_rows % STRIP or width % 128 or planes > 64:
+    if nx % 2 or ny % 2 or nx < 4 or ny < 4 or y_rows % STRIP or 2 * PAD % LONG or width % 128 or planes > 64:
         return 0
     if 30 * planes * y_rows * width > 64 * 2**20:
         return 0

time: 380 us -> 410 us (1.079)
  Pallas kernels: 366 us -> 398 us
    pallas_call x1, Pallas kernels: 366 us -> 398 us  [local(): pl.pallas_call(functools.partial(step_kernel, nx, ny, stages, w), out_sha...]
where the time goes in v4:
time: 410 us; the launch traced here: 406 us
  Pallas kernels  398 us (97%)
  local copies, waits for them, and re-layouts  4.47 us (1%)
    pallas_call x1, Pallas kernels, local(): pl.pallas_call(functools.partial(step_kernel, nx, ny, stages, w), out_sha...  398 us

profile of v4, /device:TPU:0, one launch (start us, length us, event | category | flops | bytes accessed | tf_op | source)
XLA Modules:
  0.0 405.8 jit_solution(712464079285542618)
XLA Ops:
  0.0 398.0 %shard_map.46 = (bf16[4,8,256,256]{3,2,1,0:T(8,128)(2,1)}, bf16[4,16,272,512]{3,2,1,0:T(8,128)(2,1)}) custom-call(f32[16,256,512]{2,1,0:T(8,128)} %phase.1, f32[16,256,512]{2,1,0:T(8,128)} %mobility.1, bf16[512,2048]{1,0:T(8,128)(2,1)} %x_hbm.1, bf16[256,2048]{1,0:T(8,128)(2,1)} %y_hbm.1), custom_call_target="tpu_custom_call" | custom-call | flops 17616076800 | bytes 83886080 | tf_op jit(solution)/shard_map/pallas_call | solution.py:533
  398.1 3.2 convert_bitcast_fusion
  401.3 4.5 %copy.6 = f32[16,2,32,8,256]{4,3,1,2,0:T(8,128)} copy(f32[16,2,32,8,256]{4,3,2,1,0:T(8,128)S(1)} %convert_bitcast_fusion) | data formatting | bytes 16777216 | tf_op jit(solution)/shard_map/convert_element_type | solution.py:564
